TPU v7x, 1024 devices: a whole 4x4x32 slice. The times are simulated.
1024 devices in a mesh: wide: 128 (over z, y_lo, core), narrow: 8 (over y_hi, x).
Axes of the slice: x: 4, y: 4 (y_hi: 2, y_lo: 2; y = y_hi * 2 + y_lo), z: 32, core: 2. Of those that a mesh axis runs over, the one named last changes fastest.
Arguments:
- tokens: bfloat16 [32768, 1024], P('wide', 'narrow'), may hold values from -6 to 6
- gate_weight: bfloat16 [1024, 14784], P('wide', 'narrow'), may hold values from -0.1875 to 0.1875
- up_weight: bfloat16 [1024, 14784], P('wide', 'narrow'), may hold values from -0.1875 to 0.1875
Outputs:
- hidden: bfloat16 [32768, 14784], P('wide', 'narrow')
All inputs are finite; a program needn't handle non-finite values.
Results may differ from a plain program's by a relative error of at most 0.001.
Values may be sent and summed in bfloat16 or wider, within the bound.
A program may use at most 32 MiB of HBM per device.

v0:
```python
import jax
import jax.numpy as jnp
from jax import lax
from jax.sharding import PartitionSpec as P


def gated(gate, up):
    return (jax.nn.silu(gate) * up).astype(jnp.bfloat16)


def local(tokens, gate_weight, up_weight):
    gathered = lax.all_gather(tokens, "narrow", axis=1, tiled=True)
    row_count = gathered.shape[0]
    width = gathered.shape[1]
    columns_dev = gate_weight.shape[1]
    gate_full = lax.all_gather(gate_weight, "wide", axis=0, tiled=True)
    up_full = lax.all_gather(up_weight, "wide", axis=0, tiled=True)
    block_rows = min(row_count, 256)
    blocks = gathered.reshape(row_count // block_rows, block_rows, width)

    def project_block(rows):
        gate = jnp.dot(rows, gate_full, preferred_element_type=jnp.float32)
        up = jnp.dot(rows, up_full, preferred_element_type=jnp.float32)
        return gated(gate, up)

    return lax.map(project_block, blocks).reshape(row_count, columns_dev)


def solution(mesh):
    in_specs = (P("wide", "narrow"), P("wide", "narrow"), P("wide", "narrow"))
    out_specs = P("wide", "narrow")
    return jax.shard_map(local, mesh=mesh, in_specs=in_specs, out_specs=out_specs, check_vma=False)
```

profile of v0, /device:TPU:1, one launch (start us, length us, event | category | flops | bytes accessed | tf_op | source)
XLA Modules:
  0.0 502.9 jit_solution(12971096522888910326)
XLA Ops:
  6.5 0.0 all-gather.3.cloned.1.call-start
  6.5 0.7 all-gather.3.cloned.1.call-update
  7.3 0.0 all-gather.5.cloned.1.call-start
  7.3 0.7 all-gather.5.cloned.1.call-update
  8.0 27.7 %all_gather.9 = bf16[256,1024]{1,0:T(8,128)(2,1)S(1)} all-gather(bf16[256,128]{1,0:T(8,128)(2,1)} %param.3), channel_id=1, replica_groups=mesh['wide'=128,'narrow'=8] {'narrow'}, dimensions={1}, use_global_device_ids=true | all-gather | bytes 589824 | tf_op jit(solution)/shard_map/all_gather | solution.py:12
  35.7 221.4 %all-gather.3.cloned.1.call-done = bf16[1024,1848]{1,0:T(8,128)(2,1)} async-done(((bf16[8,1848]{1,0:T(8,128)(2,1)}), bf16[1024,1848]{1,0:T(8,128)(2,1)}) %all-gather.3.cloned.1.call-update) | async-done | bytes 3784720 | tf_op jit(solution)/shard_map/all_gather | solution.py:16
  257.1 3.7 fusion.1
  260.9 230.4 %all-gather.5.cloned.1.call-done = bf16[1024,1848]{1,0:T(8,128)(2,1)} async-done(((bf16[8,1848]{1,0:T(8,128)(2,1)}), bf16[1024,1848]{1,0:T(8,128)(2,1)}) %all-gather.5.cloned.1.call-update) | async-done | bytes 3784720 | tf_op jit(solution)/shard_map/all_gather | solution.py:17
  491.3 4.7 fusion
Async XLA Ops:
  6.5 250.6 %all-gather.3.cloned.1.call-start = ((), (), s32[]{:S(2)}) async-start(), calls=%async_computation | async-start | bytes 3962880 | tf_op jit(solution)/shard_map/all_gather | solution.py:16
  7.3 484.0 %all-gather.5.cloned.1.call-start = ((), (), s32[]{:S(2)}) async-start(), calls=%async_computation.1 | async-start | bytes 3962880 | tf_op jit(solution)/shard_map/all_gather | solution.py:17
Sparse Core Ops, SparseCore 0:
  10.1 246.9 all-gather.2
  259.9 231.3 all-gather.4
where the time goes:
time: 503 us
  waiting for transfers between devices  453 us (90%)
  blocking collectives  27.7 us (6%)
  between operations  13.4 us (3%)
  matrix products  8.47 us (2%)
    all_gather x1, waiting for transfers between devices, local(): up_full = lax.all_gather(up_weight, 'wide', axis=0, tiled=True)  230 us
    all_gather x1, waiting for transfers between devices, local(): gate_full = lax.all_gather(gate_weight, 'wide', axis=0, tiled=True)  221 us
    all_gather x1, blocking collectives, local(): gathered = lax.all_gather(tokens, 'narrow', axis=1, tiled=True)  27.7 us
  transfers between devices with their start and end apart: 2, of which 2 were waited for; matrix products, arithmetic and copies ran while one was open for 1% of the time, Pallas kernels for 0%

commit v1 on v0

v1 whole, which is shorter than its diff:
```python
import functools
import jax
import jax.numpy as jnp
from jax import lax
from jax.experimental import pallas as pl
from jax.experimental.pallas import tpu as pltpu
from jax.sharding import PartitionSpec as P

MESH = pl.DeviceIdType.MESH
QUAD = 4
XS = 4
YS = 4
LANES = 512
CHUNKS = 2
LAG = 5.0
STRIDE = 2


def tree(planes, stride):
    right, left = planes // 2, planes - planes // 2 - 1
    parent = {}
    for sign, reach in ((1, right), (-1, left)):
        for t in range(1, reach + 1):
            parent[sign * t] = sign * (t - stride if t % stride == 0 else t - 1)
    return parent


def plan(parent):
    children = {}
    for t, p in parent.items():
        children.setdefault(p, []).append(t)
    due = {0: 0.0}

    def walk(p):
        for i, t in enumerate(children.get(p, [])):
            due[t] = due[p] + 1.8 + 0.6 * abs(t - p) + 0.3 * i
            walk(t)

    for p in children:
        children[p].sort(key=lambda t: (-abs(t - p), t))
    walk(0)
    return children, due


def kernel(
    planes, tok_ref, gate_ref, up_ref, out_ref, toks, stage, quads, weights, result, tok_send, tok_recv,
    quad_send, quad_recv, item_send, item_recv, out_send, out_recv,
):
    w, n = lax.axis_index("wide"), lax.axis_index("narrow")
    z, q = w // QUAD, w % QUAD
    core, x, y_hi, y_lo = q % 2, n % XS, n // XS, q // 2
    y = y_hi * 2 + y_lo
    parent = tree(planes, STRIDE)
    children, due = plan(parent)
    steps = sorted({t - p for t, p in parent.items()})
    steps = sorted(set(steps) | {-s for s in steps})
    each = LANES // CHUNKS

    def plane_dev(dz):
        return (lax.rem(z + dz + 2 * planes, planes) * QUAD + q, n)

    def quad_dev(k):
        return (z * QUAD + (q ^ k), n)

    def y_dev(dy):
        yy = lax.rem(y + dy, YS)
        return (z * QUAD + lax.rem(yy, 2) * 2 + core, (yy // 2) * XS + x)

    def x_dev(dx):
        return (w, y_hi * XS + lax.rem(x + dx + XS, XS))

    barrier = pltpu.get_barrier_semaphore()
    peers = [plane_dev(s) for s in steps] + [quad_dev(k) for k in (1, 2, 3)]
    peers += [y_dev(d) for d in (1, 2, 3)] + [x_dev(1), x_dev(-1)]
    for peer in peers:
        pl.semaphore_signal(barrier, inc=1, device_id=peer, device_id_type=MESH)

    full = gate_ref.shape[1]
    for k in range(QUAD):
        size = min(LANES, full - k * LANES)
        both = jnp.concatenate(
            [r[:, k * LANES : k * LANES + size].astype(jnp.float32) for r in (gate_ref, up_ref)], axis=0
        )
        if size < LANES:
            both = jnp.concatenate([both, jnp.zeros((both.shape[0], LANES - size), jnp.float32)], axis=1)
        stage[k] = both.astype(jnp.bfloat16)
    toks[core, x, y] = tok_ref[...]
    quads[q] = stage[q]
    pl.semaphore_wait(barrier, len(peers))

    def quad_copy(k):
        return pltpu.make_async_remote_copy(
            stage.at[q ^ k], quads.at[q], quad_send.at[k], quad_recv.at[k], device_id=quad_dev(k), device_id_type=MESH
        )

    for k in (3, 2, 1):
        quad_copy(k).start()

    def y_copy(d):
        block = toks.at[core, x, y]
        return pltpu.make_async_remote_copy(
            block, block, tok_send.at[d - 1], tok_recv.at[d - 1], device_id=y_dev(d), device_id_type=MESH
        )

    def x_copy(i):
        from_x = lax.rem(x + (0, 0, -1, 1)[i] + XS, XS)
        block = toks.at[core, from_x]
        if i >= 2:
            block = toks.at[core, from_x, pl.ds((i - 2) * 2, 2)]
        return pltpu.make_async_remote_copy(
            block, block, tok_send.at[3 + i], tok_recv.at[3 + i], device_id=x_dev((1, -1, 1, -1)[i]), device_id_type=MESH
        )

    def core_copy():
        block = toks.at[core]
        return pltpu.make_async_remote_copy(
            block, block, tok_send.at[7], tok_recv.at[7], device_id=quad_dev(1), device_id_type=MESH
        )

    for d in (1, 2, 3):
        y_copy(d).start()

    for k in (1, 2, 3):
        quad_copy(k).wait_recv()
    rows = [quads[s].astype(jnp.float32) for s in range(QUAD)]
    half = rows[0].shape[0] // 2
    gate_rows = jnp.concatenate([r[:half] for r in rows], axis=0).astype(jnp.bfloat16)
    up_rows = jnp.concatenate([r[half:] for r in rows], axis=0).astype(jnp.bfloat16)
    for c in range(CHUNKS):
        weights[c, z] = jnp.concatenate(
            [gate_rows[:, c * each : (c + 1) * each], up_rows[:, c * each : (c + 1) * each]], axis=1
        )

    order = sorted(((due[t] + c * LAG, c, t) for t in due for c in range(CHUNKS)))
    place = {t: i for i, t in enumerate(sorted(due))}

    def item_copy(at, to, c):
        item = weights.at[c, lax.rem(z - at + 2 * planes, planes)]
        return pltpu.make_async_remote_copy(
            item, item, item_send.at[c, place[to]], item_recv.at[c, place[to]],
            device_id=plane_dev(to - at), device_id_type=MESH,
        )

    def out_copy(c, k):
        columns = pl.ds(pl.multiple_of(q * LANES + c * each, 128), each)
        return pltpu.make_async_remote_copy(
            result.at[c, k - 1], out_ref.at[:, columns], out_send.at[c, k - 1], out_recv.at[c, k - 1],
            device_id=quad_dev(k), device_id_type=MESH,
        )

    def from_peer(c, k):
        columns = pl.ds(pl.multiple_of((q ^ k) * LANES + c * each, 128), each)
        return pltpu.make_async_remote_copy(
            result.at[c, k - 1], out_ref.at[:, columns], out_send.at[c, k - 1], out_recv.at[c, k - 1],
            device_id=quad_dev(k), device_id_type=MESH,
        )

    def compute(c):
        depth = planes * weights.shape[2]
        for k in (3, 2, 1, 0):
            row = q ^ k
            r_core, r_lo = row % 2, row // 2
            left = jnp.concatenate(
                [toks[r_core, i % XS, (i // XS) * 2 + r_lo] for i in range(2 * XS)], axis=1
            )
            right = weights[c].reshape(depth, 2 * each)
            both = jnp.dot(left, right, preferred_element_type=jnp.float32)
            gate, up = both[:, :each], both[:, each:]
            hidden = (gate / (1.0 + jnp.exp(-gate)) * up).astype(jnp.bfloat16)
            if k == 0:
                out_ref[:, pl.ds(pl.multiple_of(q * LANES + c * each, 128), each)] = hidden
            else:
                result[c, k - 1] = hidden
                out_copy(c, k).start()

    left_over = [sum(1 for _, cc, t in order if cc == c and t != 0) for c in range(CHUNKS)]
    others = [(2.0, "y"), (7.0, "x"), (13.0, "core"), (17.0, "end")]
    for when, c, t in order:
        while others and when >= others[0][0]:
            token_step(others.pop(0)[1], y_copy, x_copy, core_copy)
        if t != 0:
            item_copy(parent[t], t, c).wait_recv()
            left_over[c] -= 1
        for child in children.get(t, []):
            item_copy(t, child, c).start()
        if left_over[c] == 0:
            while others:
                token_step(others.pop(0)[1], y_copy, x_copy, core_copy)
            compute(c)

    for c in range(CHUNKS):
        for k in (1, 2, 3):
            from_peer(c, k).wait_recv()
            out_copy(c, k).wait_send()
    for k in (1, 2, 3):
        quad_copy(k).wait_send()
        y_copy(k).wait_send()
    for i in range(4):
        x_copy(i).wait_send()
    core_copy().wait_send()
    for _, c, t in order:
        for child in children.get(t, []):
            item_copy(t, child, c).wait_send()


def token_step(name, y_copy, x_copy, core_copy):
    if name == "y":
        for d in (1, 2, 3):
            y_copy(d).wait_recv()
        x_copy(0).start()
        x_copy(1).start()
    elif name == "x":
        x_copy(0).wait_recv()
        x_copy(2).start()
        x_copy(1).wait_recv()
        x_copy(3).start()
    elif name == "core":
        x_copy(2).wait_recv()
        x_copy(3).wait_recv()
        core_copy().start()
    else:
        core_copy().wait_recv()


def local(planes, tokens, gate_weight, up_weight):
    rows, depth_part = tokens.shape
    each = LANES // CHUNKS
    full = gate_weight.shape[1]
    dma = pltpu.SemaphoreType.DMA
    padded = pl.pallas_call(
        functools.partial(kernel, planes),
        out_shape=jax.ShapeDtypeStruct((rows, QUAD * LANES), jnp.bfloat16),
        in_specs=[pl.BlockSpec(memory_space=pltpu.VMEM)] * 3,
        out_specs=pl.BlockSpec(memory_space=pltpu.VMEM),
        scratch_shapes=[
            pltpu.VMEM((2, XS, YS, rows, depth_part), jnp.bfloat16),
            pltpu.VMEM((QUAD, 2 * gate_weight.shape[0], LANES), jnp.bfloat16),
            pltpu.VMEM((QUAD, 2 * gate_weight.shape[0], LANES), jnp.bfloat16),
            pltpu.VMEM((CHUNKS, planes, QUAD * gate_weight.shape[0], 2 * each), jnp.bfloat16),
            pltpu.VMEM((CHUNKS, QUAD - 1, rows, each), jnp.bfloat16),
            dma((8,)),
            dma((8,)),
            dma((QUAD,)),
            dma((QUAD,)),
            dma((CHUNKS, planes)),
            dma((CHUNKS, planes)),
            dma((CHUNKS, QUAD - 1)),
            dma((CHUNKS, QUAD - 1)),
        ],
        compiler_params=pltpu.CompilerParams(collective_id=0, has_side_effects=True, vmem_limit_bytes=40 << 20),
        cost_estimate=pl.CostEstimate(flops=4 * rows * 1024 * full, bytes_accessed=1 << 23, transcendentals=rows * full),
    )(tokens, gate_weight, up_weight)
    return padded[:, :full]


def solution(mesh):
    spec = P("wide", "narrow")
    planes = mesh.shape["wide"] // QUAD
    return jax.shard_map(
        functools.partial(local, planes), mesh=mesh, in_specs=(spec, spec, spec), out_specs=spec, check_vma=False
    )
```

time: 503 us -> 77.1 us (0.15)
  waiting for transfers between devices: 453 us -> 0 us
  Pallas kernels: 0 us -> 72.4 us
  blocking collectives: 27.7 us -> 0 us
  between operations: 13.4 us -> 0.02 us
  matrix products: 8.47 us -> 0 us
    all_gather x2 -> x0, waiting for transfers between devices: 452 us -> none  [the longest x1 230 us: local(): up_full = lax.all_gather(up_weight, 'wide', axis=0, tiled=True)]
    pallas_call x0 -> x1, Pallas kernels: none -> 72.4 us  [local(): pl.pallas_call(functools.partial(kernel, planes), out_shape=jax.ShapeDtyp...]
    all_gather x1 -> x0, blocking collectives: 27.7 us -> none  [local(): gathered = lax.all_gather(tokens, 'narrow', axis=1, tiled=True)]
    dot_general x2 -> x0, matrix products: 8.47 us -> none  [the longest x1 4.72 us: project_block(): up = jnp.dot(rows, up_full, preferred_element_type=jnp.float32)]
  transfers between devices with their start and end apart: 2 -> 0, of which waited for: 2 -> 0; matrix products, arithmetic and copies ran while one was open for 1% -> 0% of each run, Pallas kernels for 0% -> 0%
where the time goes in v1:
time: 77.1 us; the launch traced here: 76.1 us
  Pallas kernels  72.4 us (94%)
  local copies, waits for them, and re-layouts  3.7 us (5%)
    pallas_call x1, Pallas kernels, local(): pl.pallas_call(functools.partial(kernel, planes), out_shape=jax.ShapeDtyp...  72.4 us
    unnamed x6, local copies, waits for them, and re-layouts  2.34 us

profile of v1, /device:TPU:1, one launch (start us, length us, event | category | flops | bytes accessed | tf_op | source)
XLA Modules:
  0.0 76.1 jit_solution(10586268417620929197)
XLA Ops:
  0.0 0.0 copy-start
  0.0 0.8 %copy-done = bf16[256,128]{1,0:T(8,128)(2,1)S(1)} copy-done((bf16[256,128]{1,0:T(8,128)(2,1)S(1)}, bf16[256,128]{1,0:T(8,128)(2,1)}, u32[]{:S(2)}) %copy-start) | copy-done | bytes 65560
  0.8 0.0 copy-start.1
  0.8 0.8 copy-done.1
  1.6 0.0 copy-start.2
  1.6 0.8 copy-done.2
  2.3 72.4 %shard_map.37 = bf16[256,2048]{1,0:T(8,128)(2,1)S(1)} custom-call(bf16[256,128]{1,0:T(8,128)(2,1)S(1)} %copy-done, bf16[8,1848]{1,0:T(8,128)(2,1)S(1)} %copy-done.1, bf16[8,1848]{1,0:T(8,128)(2,1)S(1)} %copy-done.2), custom_call_target="tpu_custom_call" | custom-call | flops 1937768448 | bytes 8388608 | tf_op jit(solution)/shard_map/pallas_call | solution.py:230
  74.7 0.1 slice.3
  74.8 1.3 %copy.4 = bf16[256,1848]{0,1:T(8,128)(2,1)} copy(bf16[256,1848]{1,0:T(8,128)(2,1)S(1)} %slice.3) | data formatting | bytes 1892352 | tf_op jit(solution)/shard_map/slice | solution.py:253
Async XLA Ops:
  0.0 0.8 %copy-start = (bf16[256,128]{1,0:T(8,128)(2,1)S(1)}, bf16[256,128]{1,0:T(8,128)(2,1)}, u32[]{:S(2)}) copy-start(bf16[256,128]{1,0:T(8,128)(2,1)} %tok_ref.1) | copy-start | bytes 196612
  0.8 0.8 copy-start.1
  1.6 0.8 copy-start.2

commit v2 on v1

v2 whole, which is shorter than its diff:
```python
import functools
import jax
import jax.numpy as jnp
from jax import lax
from jax.experimental import pallas as pl
from jax.experimental.pallas import tpu as pltpu
from jax.sharding import PartitionSpec as P

MESH = pl.DeviceIdType.MESH
TEAM = 8
XS = 4
YS = 4
LANES = 256
CHUNKS = 2
LAG = 0.7
STRIDE = 1
STAGE = 4.2


def tree(planes, stride):
    right, left = planes // 2, planes - planes // 2 - 1
    parent = {}
    for sign, reach in ((1, right), (-1, left)):
        for t in range(1, reach + 1):
            parent[sign * t] = sign * (t - stride if t % stride == 0 else t - 1)
    return parent


def plan(parent):
    children = {}
    for t, p in parent.items():
        children.setdefault(p, []).append(t)
    due = {0: 0.0}

    def walk(p):
        for i, t in enumerate(children.get(p, [])):
            due[t] = due[p] + STAGE * abs(t - p) + 0.1 * i
            walk(t)

    for p in children:
        children[p].sort(key=lambda t: (-abs(t - p), t))
    walk(0)
    return children, due


def kernel(
    planes, tok_hbm, gate_hbm, up_hbm, out_ref, toks, gate_ref, up_ref, stage, quads, weights, result, load_sem, tok_send, tok_recv,
    quad_send, quad_recv, item_send, item_recv, out_send, out_recv,
):
    w, n = lax.axis_index("wide"), lax.axis_index("narrow")
    z, q = w // TEAM, w % TEAM
    core, x, y_hi, y_lo, side = q % 2, n % XS, n // XS, (q // 2) % 2, q // 4
    y = y_hi * 2 + y_lo
    parent = tree(planes, STRIDE)
    children, due = plan(parent)
    steps = sorted({t - p for t, p in parent.items()})
    steps = sorted(set(steps) | {-s for s in steps})
    each = LANES // CHUNKS

    def plane_dev(dz):
        return (lax.rem(z + dz + 2 * planes, planes) * TEAM + q, n)

    def quad_dev(k):
        return (z * TEAM + (q ^ k), n)

    def y_dev(dy):
        yy = lax.rem(y + dy, YS)
        return (z * TEAM + side * 4 + lax.rem(yy, 2) * 2 + core, (yy // 2) * XS + x)

    def x_dev(dx):
        return (w, y_hi * XS + lax.rem(x + dx + XS, XS))

    barrier = pltpu.get_barrier_semaphore()
    peers = [plane_dev(s) for s in steps] + [quad_dev(k) for k in range(1, TEAM)]
    peers += [y_dev(d) for d in (1, 2, 3)] + [x_dev(1), x_dev(-1)]
    for peer in peers:
        pl.semaphore_signal(barrier, inc=1, device_id=peer, device_id_type=MESH)

    loads = [
        pltpu.make_async_copy(gate_hbm, gate_ref, load_sem.at[0]),
        pltpu.make_async_copy(up_hbm, up_ref, load_sem.at[1]),
        pltpu.make_async_copy(tok_hbm, toks.at[core, x, y, side], load_sem.at[2]),
    ]
    for load in loads:
        load.start()
    loads[0].wait()
    loads[1].wait()

    full = gate_ref.shape[1]
    for k in range(TEAM):
        size = min(LANES, full - k * LANES)
        both = jnp.concatenate(
            [r[:, k * LANES : k * LANES + size].astype(jnp.float32) for r in (gate_ref, up_ref)], axis=0
        )
        if size < LANES:
            both = jnp.concatenate([both, jnp.zeros((both.shape[0], LANES - size), jnp.float32)], axis=1)
        stage[k] = both.astype(jnp.bfloat16)
    quads[q] = stage[q]
    loads[2].wait()
    pl.semaphore_wait(barrier, len(peers))

    def side_copy():
        block = toks.at[core, x, y, side]
        return pltpu.make_async_remote_copy(
            block, block, tok_send.at[0], tok_recv.at[0], device_id=quad_dev(4), device_id_type=MESH
        )

    def quad_copy(k):
        return pltpu.make_async_remote_copy(
            stage.at[q ^ k], quads.at[q], quad_send.at[k], quad_recv.at[k], device_id=quad_dev(k), device_id_type=MESH
        )

    for k in (6, 7, 4, 5, 2, 3, 1):
        quad_copy(k).start()
    side_copy().start()

    def y_copy(d):
        block = toks.at[core, x, y]
        return pltpu.make_async_remote_copy(
            block, block, tok_send.at[d], tok_recv.at[d], device_id=y_dev(d), device_id_type=MESH
        )

    def x_copy(i):
        from_x = lax.rem(x + (0, 0, -1, 1)[i] + XS, XS)
        block = toks.at[core, from_x]
        if i >= 2:
            block = toks.at[core, from_x, pl.ds((i - 2) * 2, 2)]
        return pltpu.make_async_remote_copy(
            block, block, tok_send.at[4 + i], tok_recv.at[4 + i], device_id=x_dev((1, -1, 1, -1)[i]), device_id_type=MESH
        )

    def core_copy(i):
        block = toks.at[core, lax.rem(x + i, XS)]
        return pltpu.make_async_remote_copy(
            block, block, tok_send.at[8 + i], tok_recv.at[8 + i], device_id=quad_dev(1), device_id_type=MESH
        )

    for k in range(1, TEAM):
        quad_copy(k).wait_recv()
    rows = [quads[s].astype(jnp.float32) for s in range(TEAM)]
    half = rows[0].shape[0] // 2
    gate_rows = jnp.concatenate([r[:half] for r in rows], axis=0).astype(jnp.bfloat16)
    up_rows = jnp.concatenate([r[half:] for r in rows], axis=0).astype(jnp.bfloat16)
    for c in range(CHUNKS):
        weights[c, z] = jnp.concatenate(
            [gate_rows[:, c * each : (c + 1) * each], up_rows[:, c * each : (c + 1) * each]], axis=1
        )

    order = sorted(((due[t] + c * LAG, c, t) for t in due for c in range(CHUNKS)))
    place = {t: i for i, t in enumerate(sorted(due))}

    def item_copy(at, to, c):
        item = weights.at[c, lax.rem(z - at + 2 * planes, planes)]
        return pltpu.make_async_remote_copy(
            item, item, item_send.at[c, place[to]], item_recv.at[c, place[to]],
            device_id=plane_dev(to - at), device_id_type=MESH,
        )

    def out_copy(c, k):
        units = pl.ds(pl.multiple_of(q * LANES + c * each, 128), each)
        return pltpu.make_async_remote_copy(
            result.at[c, k], out_ref.at[units], out_send.at[c, k], out_recv.at[c, k],
            device_id=quad_dev(k), device_id_type=MESH,
        )

    def own_copy(c):
        units = pl.ds(pl.multiple_of(q * LANES + c * each, 128), each)
        return pltpu.make_async_copy(result.at[c, 0], out_ref.at[units], out_send.at[c, 0])

    def from_peer(c, k):
        units = pl.ds(pl.multiple_of((q ^ k) * LANES + c * each, 128), each)
        return pltpu.make_async_remote_copy(
            result.at[c, k], out_ref.at[units], out_send.at[c, k], out_recv.at[c, k],
            device_id=quad_dev(k), device_id_type=MESH,
        )

    def compute(c):
        depth = planes * weights.shape[2]
        right = weights[c].reshape(depth, 2 * each).T
        for k in (7, 6, 3, 2, 5, 4, 1, 0):
            row = q ^ k
            r_core, r_lo, r_side = row % 2, (row // 2) % 2, row // 4
            left = jnp.concatenate(
                [toks[r_core, i % XS, (i // XS) * 2 + r_lo, r_side] for i in range(2 * XS)], axis=1
            )
            both = lax.dot_general(right, left, (((1,), (1,)), ((), ())), preferred_element_type=jnp.float32)
            gate, up = both[:each], both[each:]
            hidden = (gate / (1.0 + jnp.exp(-gate)) * up).astype(jnp.bfloat16)
            result[c, k] = hidden
            own_copy(c).start() if k == 0 else out_copy(c, k).start()

    left_over = [sum(1 for _, cc, t in order if cc == c and t != 0) for c in range(CHUNKS)]
    others = [(2.5, "y"), (6.0, "x"), (21.0, "x2"), (27.0, "core"), (31.0, "end")]
    for when, c, t in order:
        while others and when >= others[0][0]:
            token_step(others.pop(0)[1], side_copy, y_copy, x_copy, core_copy)
        if t != 0:
            item_copy(parent[t], t, c).wait_recv()
            left_over[c] -= 1
        for child in children.get(t, []):
            item_copy(t, child, c).start()
        if left_over[c] == 0:
            while others:
                token_step(others.pop(0)[1], side_copy, y_copy, x_copy, core_copy)
            compute(c)

    for k in range(1, TEAM):
        quad_copy(k).wait_send()
    side_copy().wait_send()
    for d in (1, 2, 3):
        y_copy(d).wait_send()
    for i in range(4):
        x_copy(i).wait_send()
        core_copy(i).wait_send()
    for _, c, t in order:
        for child in children.get(t, []):
            item_copy(t, child, c).wait_send()
    for c in range(CHUNKS):
        for k in range(1, TEAM):
            from_peer(c, k).wait_recv()
            out_copy(c, k).wait_send()
        own_copy(c).wait()


def token_step(name, side_copy, y_copy, x_copy, core_copy):
    if name == "y":
        side_copy().wait_recv()
        for d in (1, 2, 3):
            y_copy(d).start()
    elif name == "x":
        for d in (1, 2, 3):
            y_copy(d).wait_recv()
        x_copy(0).start()
        x_copy(1).start()
        core_copy(0).start()
    elif name == "x2":
        x_copy(0).wait_recv()
        x_copy(2).start()
        core_copy(3).start()
        x_copy(1).wait_recv()
        x_copy(3).start()
        core_copy(1).start()
    elif name == "core":
        x_copy(2).wait_recv()
        x_copy(3).wait_recv()
        core_copy(2).start()
    else:
        for i in range(4):
            core_copy(i).wait_recv()


def local(planes, tokens, gate_weight, up_weight):
    rows, depth_part = tokens.shape
    each = LANES // CHUNKS
    full = gate_weight.shape[1]
    dma = pltpu.SemaphoreType.DMA
    padded = pl.pallas_call(
        functools.partial(kernel, planes),
        out_shape=jax.ShapeDtypeStruct((TEAM * LANES, rows), jnp.bfloat16),
        in_specs=[pl.BlockSpec(memory_space=pltpu.HBM)] * 3,
        out_specs=pl.BlockSpec(memory_space=pltpu.HBM),
        scratch_shapes=[
            pltpu.VMEM((2, XS, YS, 2, rows, depth_part), jnp.bfloat16),
            pltpu.VMEM(gate_weight.shape, jnp.bfloat16),
            pltpu.VMEM(up_weight.shape, jnp.bfloat16),
            pltpu.VMEM((TEAM, 2 * gate_weight.shape[0], LANES), jnp.bfloat16),
            pltpu.VMEM((TEAM, 2 * gate_weight.shape[0], LANES), jnp.bfloat16),
            pltpu.VMEM((CHUNKS, planes, TEAM * gate_weight.shape[0], 2 * each), jnp.bfloat16),
            pltpu.VMEM((CHUNKS, TEAM, each, rows), jnp.bfloat16),
            dma((3,)),
            dma((12,)),
            dma((12,)),
            dma((TEAM,)),
            dma((TEAM,)),
            dma((CHUNKS, planes)),
            dma((CHUNKS, planes)),
            dma((CHUNKS, TEAM)),
            dma((CHUNKS, TEAM)),
        ],
        compiler_params=pltpu.CompilerParams(collective_id=0, has_side_effects=True, vmem_limit_bytes=61 << 20),
        cost_estimate=pl.CostEstimate(flops=4 * rows * 1024 * full, bytes_accessed=1 << 23, transcendentals=rows * full),
    )(tokens, gate_weight, up_weight)
    return padded[:full].T


def solution(mesh):
    spec = P("wide", "narrow")
    planes = mesh.shape["wide"] // TEAM
    return jax.shard_map(
        functools.partial(local, planes), mesh=mesh, in_specs=(spec, spec, spec), out_specs=spec, check_vma=False
    )
```

time: 77.1 us -> 74 us (0.960); the launches traced: 76.1 us -> 73.8 us
  local copies, waits for them, and re-layouts: 3.7 us -> 2.18 us
  Pallas kernels: 72.4 us -> 71.6 us
    unnamed x6 -> x0, local copies, waits for them, and re-layouts: 2.34 us -> none
    transpose x0 -> x1, local copies, waits for them, and re-layouts: none -> 2.18 us  [local(): return padded[:full].T]
    slice x2 -> x0, local copies, waits for them, and re-layouts: 1.36 us -> none  [local(): return padded[:, :full]]
    pallas_call x1, Pallas kernels: 72.4 us -> 71.6 us  [local(): pl.pallas_call(functools.partial(kernel, planes), out_shape=jax.ShapeDtyp...]
where the time goes in v2:
time: 74 us; the launch traced here: 73.8 us
  Pallas kernels  71.6 us (97%)
  local copies, waits for them, and re-layouts  2.18 us (3%)
    pallas_call x1, Pallas kernels, local(): pl.pallas_call(functools.partial(kernel, planes), out_shape=jax.ShapeDtyp...  71.6 us
    transpose x1, local copies, waits for them, and re-layouts, local(): return padded[:full].T  2.18 us

profile of v2, /device:TPU:1, one launch (start us, length us, event | category | flops | bytes accessed | tf_op | source)
XLA Modules:
  0.0 73.8 jit_solution(11619577574242916572)
XLA Ops:
  0.0 71.6 %shard_map.37 = bf16[2048,256]{1,0:T(8,128)(2,1)} custom-call(bf16[256,128]{1,0:T(8,128)(2,1)} %tok_hbm.1, bf16[8,1848]{1,0:T(8,128)(2,1)} %gate_hbm.1, bf16[8,1848]{1,0:T(8,128)(2,1)} %up_hbm.1), custom_call_target="tpu_custom_call" | custom-call | flops 1937768448 | bytes 8388608 | tf_op jit(solution)/shard_map/pallas_call | solution.py:257
  71.6 2.2 %slice_bitcast_fusion = bf16[256,1848]{0,1:T(8,128)(2,1)} fusion(bf16[2048,256]{1,0:T(8,128)(2,1)} %shard_map.37), kind=kLoop, calls=%fused_computation | loop fusion | bytes 1892352 | tf_op jit(solution)/shard_map/transpose | solution.py:283

commit v3 on v2

--- a/solution.py
+++ b/solution.py
@@ -10,19 +10,17 @@
 TEAM = 8
 XS = 4
 YS = 4
+UNITS = 240
 LANES = 256
 CHUNKS = 2
 LAG = 0.7
-STRIDE = 1
 STAGE = 4.2
 
 
-def tree(planes, stride):
-    right, left = planes // 2, planes - planes // 2 - 1
-    parent = {}
-    for sign, reach in ((1, right), (-1, left)):
-        for t in range(1, reach + 1):
-            parent[sign * t] = sign * (t - stride if t % stride == 0 else t - 1)
+def tree(planes, c):
+    right = planes // 2 - c % 2
+    parent = {t: t - 1 for t in range(1, right + 1)}
+    parent.update({-t: 1 - t for t in range(1, planes - right)})
     return parent
 
 
@@ -51,10 +49,8 @@
     z, q = w // TEAM, w % TEAM
     core, x, y_hi, y_lo, side = q % 2, n % XS, n // XS, (q // 2) % 2, q // 4
     y = y_hi * 2 + y_lo
-    parent = tree(planes, STRIDE)
-    children, due = plan(parent)
-    steps = sorted({t - p for t, p in parent.items()})
-    steps = sorted(set(steps) | {-s for s in steps})
+    parents = [tree(planes, c) for c in range(CHUNKS)]
+    plans = [plan(parent) for parent in parents]
     each = LANES // CHUNKS
 
     def plane_dev(dz):
@@ -71,7 +67,7 @@
         return (w, y_hi * XS + lax.rem(x + dx + XS, XS))
 
     barrier = pltpu.get_barrier_semaphore()
-    peers = [plane_dev(s) for s in steps] + [quad_dev(k) for k in range(1, TEAM)]
+    peers = [plane_dev(1), plane_dev(-1)] + [quad_dev(k) for k in range(1, TEAM)]
     peers += [y_dev(d) for d in (1, 2, 3)] + [x_dev(1), x_dev(-1)]
     for peer in peers:
         pl.semaphore_signal(barrier, inc=1, device_id=peer, device_id_type=MESH)
@@ -88,9 +84,9 @@
 
     full = gate_ref.shape[1]
     for k in range(TEAM):
-        size = min(LANES, full - k * LANES)
+        size = min(UNITS, full - k * UNITS)
         both = jnp.concatenate(
-            [r[:, k * LANES : k * LANES + size].astype(jnp.float32) for r in (gate_ref, up_ref)], axis=0
+            [r[:, k * UNITS : k * UNITS + size].astype(jnp.float32) for r in (gate_ref, up_ref)], axis=0
         )
         if size < LANES:
             both = jnp.concatenate([both, jnp.zeros((both.shape[0], LANES - size), jnp.float32)], axis=1)
@@ -146,8 +142,8 @@
             [gate_rows[:, c * each : (c + 1) * each], up_rows[:, c * each : (c + 1) * each]], axis=1
         )
 
-    order = sorted(((due[t] + c * LAG, c, t) for t in due for c in range(CHUNKS)))
-    place = {t: i for i, t in enumerate(sorted(due))}
+    order = sorted((due + c * LAG, c, t) for c in range(CHUNKS) for t, due in plans[c][1].items())
+    place = {t: t + planes // 2 for t in range(-planes // 2, planes // 2 + 1)}
 
     def item_copy(at, to, c):
         item = weights.at[c, lax.rem(z - at + 2 * planes, planes)]
@@ -156,21 +152,24 @@
             device_id=plane_dev(to - at), device_id_type=MESH,
         )
 
+    def made(c):
+        return min(each, UNITS - c * each)
+
     def out_copy(c, k):
-        units = pl.ds(pl.multiple_of(q * LANES + c * each, 128), each)
-        return pltpu.make_async_remote_copy(
-            result.at[c, k], out_ref.at[units], out_send.at[c, k], out_recv.at[c, k],
+        units = pl.ds(pl.multiple_of(q * UNITS + c * each, 16), made(c))
+        return pltpu.make_async_remote_copy(
+            result.at[c, k, pl.ds(0, made(c))], out_ref.at[units], out_send.at[c, k], out_recv.at[c, k],
             device_id=quad_dev(k), device_id_type=MESH,
         )
 
     def own_copy(c):
-        units = pl.ds(pl.multiple_of(q * LANES + c * each, 128), each)
-        return pltpu.make_async_copy(result.at[c, 0], out_ref.at[units], out_send.at[c, 0])
+        units = pl.ds(pl.multiple_of(q * UNITS + c * each, 16), made(c))
+        return pltpu.make_async_copy(result.at[c, 0, pl.ds(0, made(c))], out_ref.at[units], out_send.at[c, 0])
 
     def from_peer(c, k):
-        units = pl.ds(pl.multiple_of((q ^ k) * LANES + c * each, 128), each)
-        return pltpu.make_async_remote_copy(
-            result.at[c, k], out_ref.at[units], out_send.at[c, k], out_recv.at[c, k],
+        units = pl.ds(pl.multiple_of((q ^ k) * UNITS + c * each, 16), made(c))
+        return pltpu.make_async_remote_copy(
+            result.at[c, k, pl.ds(0, made(c))], out_ref.at[units], out_send.at[c, k], out_recv.at[c, k],
             device_id=quad_dev(k), device_id_type=MESH,
         )
 
@@ -195,9 +194,9 @@
         while others and when >= others[0][0]:
             token_step(others.pop(0)[1], side_copy, y_copy, x_copy, core_copy)
         if t != 0:
-            item_copy(parent[t], t, c).wait_recv()
+            item_copy(parents[c][t], t, c).wait_recv()
             left_over[c] -= 1
-        for child in children.get(t, []):
+        for child in plans[c][0].get(t, []):
             item_copy(t, child, c).start()
         if left_over[c] == 0:
             while others:
@@ -213,7 +212,7 @@
         x_copy(i).wait_send()
         core_copy(i).wait_send()
     for _, c, t in order:
-        for child in children.get(t, []):
+        for child in plans[c][0].get(t, []):
             item_copy(t, child, c).wait_send()
     for c in range(CHUNKS):
         for k in range(1, TEAM):
@@ -256,7 +255,7 @@
     dma = pltpu.SemaphoreType.DMA
     padded = pl.pallas_call(
         functools.partial(kernel, planes),
-        out_shape=jax.ShapeDtypeStruct((TEAM * LANES, rows), jnp.bfloat16),
+        out_shape=jax.ShapeDtypeStruct((TEAM * UNITS, rows), jnp.bfloat16),
         in_specs=[pl.BlockSpec(memory_space=pltpu.HBM)] * 3,
         out_specs=pl.BlockSpec(memory_space=pltpu.HBM),
         scratch_shapes=[
@@ -272,8 +271,8 @@
             dma((12,)),
             dma((TEAM,)),
             dma((TEAM,)),
-            dma((CHUNKS, planes)),
-            dma((CHUNKS, planes)),
+            dma((CHUNKS, planes + 1)),
+            dma((CHUNKS, planes + 1)),
             dma((CHUNKS, TEAM)),
             dma((CHUNKS, TEAM)),
         ],

time: 74 us -> 73.1 us (0.988)
  Pallas kernels: 71.6 us -> 70.7 us
    pallas_call x1, Pallas kernels: 71.6 us -> 70.7 us  [local(): pl.pallas_call(functools.partial(kernel, planes), out_shape=jax.ShapeDtyp...]
where the time goes in v3:
time: 73.1 us; the launch traced here: 72.9 us
  Pallas kernels  70.7 us (97%)
  local copies, waits for them, and re-layouts  2.18 us (3%)
    pallas_call x1, Pallas kernels, local(): pl.pallas_call(functools.partial(kernel, planes), out_shape=jax.ShapeDtyp...  70.7 us
    transpose x1, local copies, waits for them, and re-layouts, local(): return padded[:full].T  2.18 us

profile of v3, /device:TPU:1, one launch (start us, length us, event | category | flops | bytes accessed | tf_op | source)
XLA Modules:
  0.0 72.9 jit_solution(11032756254771630330)
XLA Ops:
  0.0 70.7 %shard_map.37 = bf16[1920,256]{1,0:T(8,128)(2,1)} custom-call(bf16[256,128]{1,0:T(8,128)(2,1)} %tok_hbm.1, bf16[8,1848]{1,0:T(8,128)(2,1)} %gate_hbm.1, bf16[8,1848]{1,0:T(8,128)(2,1)} %up_hbm.1), custom_call_target="tpu_custom_call" | custom-call | flops 1937768448 | bytes 8388608 | tf_op jit(solution)/shard_map/pallas_call | solution.py:256
  70.7 2.2 %slice_bitcast_fusion = bf16[256,1848]{0,1:T(8,128)(2,1)} fusion(bf16[1920,256]{1,0:T(8,128)(2,1)} %shard_map.37), kind=kLoop, calls=%fused_computation | loop fusion | bytes 1892352 | tf_op jit(solution)/shard_map/transpose | solution.py:282

commit v4 on v3

--- a/solution.py
+++ b/solution.py
@@ -66,12 +66,6 @@
     def x_dev(dx):
         return (w, y_hi * XS + lax.rem(x + dx + XS, XS))
 
-    barrier = pltpu.get_barrier_semaphore()
-    peers = [plane_dev(1), plane_dev(-1)] + [quad_dev(k) for k in range(1, TEAM)]
-    peers += [y_dev(d) for d in (1, 2, 3)] + [x_dev(1), x_dev(-1)]
-    for peer in peers:
-        pl.semaphore_signal(barrier, inc=1, device_id=peer, device_id_type=MESH)
-
     loads = [
         pltpu.make_async_copy(gate_hbm, gate_ref, load_sem.at[0]),
         pltpu.make_async_copy(up_hbm, up_ref, load_sem.at[1]),
@@ -79,6 +73,12 @@
     ]
     for load in loads:
         load.start()
+    barrier = pltpu.get_barrier_semaphore()
+    peers = [plane_dev(1), plane_dev(-1)] + [quad_dev(k) for k in range(1, TEAM)]
+    peers += [y_dev(d) for d in (1, 2, 3)] + [x_dev(1), x_dev(-1)]
+    for peer in peers:
+        pl.semaphore_signal(barrier, inc=1, device_id=peer, device_id_type=MESH)
+
     loads[0].wait()
     loads[1].wait()
 
@@ -176,7 +176,7 @@
     def compute(c):
         depth = planes * weights.shape[2]
         right = weights[c].reshape(depth, 2 * each).T
-        for k in (7, 6, 3, 2, 5, 4, 1, 0):
+        for k in (7, 3, 5, 6, 2, 4, 1, 0):
             row = q ^ k
             r_core, r_lo, r_side = row % 2, (row // 2) % 2, row // 4
             left = jnp.concatenate(

time: 73.1 us -> 72.8 us (level)
  no operation moved by 1% of the time
where the time goes in v4:
time: 72.8 us; the launch traced here: 72.2 us
  Pallas kernels  70 us (96%)
  local copies, waits for them, and re-layouts  2.18 us (3%)
    pallas_call x1, Pallas kernels, local(): pl.pallas_call(functools.partial(kernel, planes), out_shape=jax.ShapeDtyp...  70 us
    transpose x1, local copies, waits for them, and re-layouts, local(): return padded[:full].T  2.18 us

profile of v4, /device:TPU:1, one launch (start us, length us, event | category | flops | bytes accessed | tf_op | source)
XLA Modules:
  0.0 72.2 jit_solution(7838927093527677982)
XLA Ops:
  0.0 70.0 %shard_map.37 = bf16[1920,256]{1,0:T(8,128)(2,1)} custom-call(bf16[256,128]{1,0:T(8,128)(2,1)} %tok_hbm.1, bf16[8,1848]{1,0:T(8,128)(2,1)} %gate_hbm.1, bf16[8,1848]{1,0:T(8,128)(2,1)} %up_hbm.1), custom_call_target="tpu_custom_call" | custom-call | flops 1937768448 | bytes 8388608 | tf_op jit(solution)/shard_map/pallas_call | solution.py:256
  70.0 2.2 %slice_bitcast_fusion = bf16[256,1848]{0,1:T(8,128)(2,1)} fusion(bf16[1920,256]{1,0:T(8,128)(2,1)} %shard_map.37), kind=kLoop, calls=%fused_computation | loop fusion | bytes 1892352 | tf_op jit(solution)/shard_map/transpose | solution.py:282

commit v5 on v4

--- a/solution.py
+++ b/solution.py
@@ -60,7 +60,7 @@
         return (z * TEAM + (q ^ k), n)
 
     def y_dev(dy):
-        yy = lax.rem(y + dy, YS)
+        yy = y ^ dy
         return (z * TEAM + side * 4 + lax.rem(yy, 2) * 2 + core, (yy // 2) * XS + x)
 
     def x_dev(dx):
@@ -75,7 +75,7 @@
         load.start()
     barrier = pltpu.get_barrier_semaphore()
     peers = [plane_dev(1), plane_dev(-1)] + [quad_dev(k) for k in range(1, TEAM)]
-    peers += [y_dev(d) for d in (1, 2, 3)] + [x_dev(1), x_dev(-1)]
+    peers += [y_dev(2), y_dev(3)] + [x_dev(1), x_dev(-1)]
     for peer in peers:
         pl.semaphore_signal(barrier, inc=1, device_id=peer, device_id_type=MESH)
 

time: 72.8 us -> 73.3 us (level)
  no operation moved by 1% of the time
where the time goes in v5:
time: 73.3 us; the launch traced here: 72.5 us
  Pallas kernels  70.4 us (96%)
  local copies, waits for them, and re-layouts  2.18 us (3%)
    pallas_call x1, Pallas kernels, local(): pl.pallas_call(functools.partial(kernel, planes), out_shape=jax.ShapeDtyp...  70.4 us
    transpose x1, local copies, waits for them, and re-layouts, local(): return padded[:full].T  2.18 us

profile of v5, /device:TPU:1, one launch (start us, length us, event | category | flops | bytes accessed | tf_op | source)
XLA Modules:
  0.0 72.5 jit_solution(15597428949958723347)
XLA Ops:
  0.0 70.4 %shard_map.37 = bf16[1920,256]{1,0:T(8,128)(2,1)} custom-call(bf16[256,128]{1,0:T(8,128)(2,1)} %tok_hbm.1, bf16[8,1848]{1,0:T(8,128)(2,1)} %gate_hbm.1, bf16[8,1848]{1,0:T(8,128)(2,1)} %up_hbm.1), custom_call_target="tpu_custom_call" | custom-call | flops 1937768448 | bytes 8388608 | tf_op jit(solution)/shard_map/pallas_call | solution.py:256
  70.4 2.2 %slice_bitcast_fusion = bf16[256,1848]{0,1:T(8,128)(2,1)} fusion(bf16[1920,256]{1,0:T(8,128)(2,1)} %shard_map.37), kind=kLoop, calls=%fused_computation | loop fusion | bytes 1892352 | tf_op jit(solution)/shard_map/transpose | solution.py:282
